TPU v7x, 128 devices: a whole 4x4x4 slice. The times are simulated.
128 devices in a mesh: grp: 8 (over x, core), dev: 16 (over y, z).
Axes of the slice: x: 4, y: 4, z: 4, core: 2. Of those that a mesh axis runs over, the one named last changes fastest.
Arguments:
- emission: float32 [64, 524288], P(None, ('grp', 'dev')), may hold values from 0.2 to 2
- positions: float32 [3, 524288], P(None, ('grp', 'dev')), may hold values from -5 to 5
- normals: float32 [3, 524288], P(None, ('grp', 'dev')), may hold values from -3 to 3
- areas: float32 [524288], P(('grp', 'dev')), may hold values from 0.5 to 4
- material: int32 [524288], P(('grp', 'dev')), may hold values from 0 to 15
- reflect: float32 [64, 16], replicated, may hold values from 0.2 to 0.8
- pair_local: int32 [16384], P(('grp', 'dev')), may hold values from 0 to 31
- pair_device: int32 [16384, 1], P(('grp', 'dev')), may hold values from 0 to 127; in each aligned block of 128 rows (0 to 127, 128 to 255, ...) at most 2 rows name the same one
- pair_block: int32 [16384], P(('grp', 'dev')), may hold values from 0 to 31
Outputs:
- radiosity: float32 [64, 524288], P(None, ('grp', 'dev'))
Inputs may be any that keep to these rules, and one draw needn't show every extreme that they name: `pair_device`: among the 128 pairs of one device, at most 2 name the same device; some device's pairs name one device exactly 2 times.
All inputs are finite; a program needn't handle non-finite values.
Results may differ from a plain program's by a relative error of at most 0.00055.
Values may be sent and summed in bfloat16 or wider, within the bound.
A program may use at most 128 MiB of HBM per device.

v0:
```python
import math

import jax
import jax.numpy as jnp
import numpy as np
from jax import lax
from jax.experimental import pallas as pl
from jax.experimental.pallas import tpu as pltpu
from jax.sharding import PartitionSpec as P

BLK = 128
SWEEPS = 2
AXES = ("grp", "dev")
DEVICES = 128
BLOCKS = 32
BANDS = 64
SLOTS = 4
CHUNKS = 4
PLACES = DEVICES // CHUNKS
TASKS = PLACES * SLOTS
MESH = pl.DeviceIdType.MESH
softening = 0.5


def torus_order():
    seen = set()
    groups = []
    for dx in range(4):
        for dy in range(4):
            for dz in range(4):
                for core in range(2):
                    group = []
                    for x, y, z in ((dx, dy, dz), (dy, dz, dx), (dz, dx, dy)):
                        for step in ((x, core, y, z), (-x % 4, core, -y % 4, -z % 4)):
                            if step not in seen and any(step):
                                seen.add(step)
                                group.append(step)
                    if group:
                        groups.append(group)
    groups.sort(key=lambda group: sum(min(v, 4 - v) for v in group[0][:1] + group[0][2:]))
    return [step for group in groups for step in group]


ORDER = torus_order()
PEERS = len(ORDER)


def peer(grp, dev, step):
    x, core, y, z = step
    return (
        lax.rem(grp // 2 + x, 4) * 2 + lax.rem(lax.rem(grp, 2) + core, 2),
        lax.rem(dev // 4 + y, 4) * 4 + lax.rem(lax.rem(dev, 4) + z, 4),
    )


def fused_kernel(
    send_index,
    mine_index,
    order_index,
    keep,
    end_index,
    has,
    emission,
    areas,
    albedo,
    geometry,
    out,
    scaled,
    total,
    running,
    send,
    send_geometry,
    recv_geometry,
    tiles0,
    tiles1,
    tiles2,
    tiles3,
    recv00,
    recv01,
    recv02,
    recv03,
    recv10,
    recv11,
    recv12,
    recv13,
    geometry_send_sem,
    geometry_recv_sem,
    send_sem,
    recv_sem,
):
    tiles = (tiles0, tiles1, tiles2, tiles3)
    recv = ((recv00, recv01, recv02, recv03), (recv10, recv11, recv12, recv13))
    grp, dev = lax.axis_index("grp"), lax.axis_index("dev")
    peers = [peer(grp, dev, step) for step in ORDER]
    barrier = pltpu.get_barrier_semaphore()
    for other in peers:
        pl.semaphore_signal(barrier, inc=1, device_id=other, device_id_type=MESH)

    def pack_geometry(place, _):
        rows = [geometry[send_index[place * SLOTS + slot]][:6] for slot in range(SLOTS)]
        send_geometry[place] = jnp.concatenate(rows, 0)
        return 0

    lax.fori_loop(0, DEVICES, pack_geometry, 0)
    recv_geometry[PEERS] = send_geometry[PEERS]

    for block in range(BLOCKS):
        lanes = pl.ds(block * BLK, BLK)
        scaled[block] = (emission[:, lanes] * areas[:, lanes]).astype(jnp.bfloat16)

    pl.semaphore_wait(barrier, PEERS)
    geometry_copies = [
        pltpu.make_async_remote_copy(
            src_ref=send_geometry.at[place],
            dst_ref=recv_geometry.at[place],
            send_sem=geometry_send_sem.at[place],
            recv_sem=geometry_recv_sem.at[place],
            device_id=other,
            device_id_type=MESH,
        )
        for place, other in enumerate(peers)
    ]
    for copy in geometry_copies:
        copy.start()

    for sweep in range(SWEEPS):

        def pack(place, _):
            for slot in range(SLOTS):
                index = place * SLOTS + slot
                send[index] = scaled[send_index[index]]
            return 0

        lax.fori_loop(0, DEVICES, pack, 0)
        for slot in range(SLOTS):
            recv[sweep][CHUNKS - 1][TASKS - SLOTS + slot] = send[PEERS * SLOTS + slot]
        copies = [
            pltpu.make_async_remote_copy(
                src_ref=send.at[pl.ds(place * SLOTS, SLOTS)],
                dst_ref=recv[sweep][place // PLACES].at[pl.ds(place % PLACES * SLOTS, SLOTS)],
                send_sem=send_sem.at[sweep * PEERS + place],
                recv_sem=recv_sem.at[sweep * PEERS + place],
                device_id=other,
                device_id_type=MESH,
            )
            for place, other in enumerate(peers)
        ]
        for copy in copies:
            copy.start()

        if sweep == 0:
            for chunk in range(CHUNKS):
                for copy in geometry_copies[chunk * PLACES : (chunk + 1) * PLACES]:
                    copy.wait_recv()

                def build(place, _):
                    far_all = recv_geometry[chunk * PLACES + place].T
                    for slot in range(SLOTS):
                        index = place * SLOTS + slot
                        near = geometry[mine_index[chunk * TASKS + index]]
                        distance_sq = softening
                        facing_near = 0.0
                        facing_far = 0.0
                        for axis in range(3):
                            column = slot * 6 + axis
                            offset = far_all[:, column : column + 1] - near[axis : axis + 1]
                            distance_sq = distance_sq + offset * offset
                            facing_near = facing_near + near[3 + axis : 4 + axis] * offset
                            facing_far = facing_far - far_all[:, column + 3 : column + 4] * offset
                        tiles[chunk][index] = (
                            jnp.maximum(facing_near, 0.0)
                            * jnp.maximum(facing_far, 0.0)
                            / (math.pi * distance_sq * distance_sq)
                        ).astype(jnp.bfloat16)
                    return 0

                lax.fori_loop(0, PLACES, build, 0)

        for chunk in range(CHUNKS):
            for copy in copies[chunk * PLACES : (chunk + 1) * PLACES]:
                copy.wait_recv()

            def add(group, run):
                for inner in range(8):
                    task = group * 8 + inner
                    index = order_index[chunk * TASKS + task]
                    run = run * keep[chunk * TASKS + task] + jnp.dot(
                        recv[sweep][chunk][index],
                        tiles[chunk][index],
                        preferred_element_type=jnp.float32,
                    )
                    running[task] = run
                return run

            lax.fori_loop(0, TASKS // 8, add, jnp.zeros((BANDS, BLK), jnp.float32))

            def fold(block, _):
                part = running[end_index[chunk * BLOCKS + block]] * has[chunk * BLOCKS + block]
                total[block] = part if chunk == 0 else total[block] + part
                return 0

            lax.fori_loop(0, BLOCKS, fold, 0)

        for copy in copies:
            copy.wait_send()
        for block in range(BLOCKS):
            lanes = pl.ds(block * BLK, BLK)
            current = emission[:, lanes] + albedo[:, lanes] * total[block]
            if sweep + 1 < SWEEPS:
                scaled[block] = (current * areas[:, lanes]).astype(jnp.bfloat16)
            else:
                out[:, lanes] = current
    for copy in geometry_copies:
        copy.wait_send()


def fused(send_index, mine_index, order_index, keep, end_index, has, emission, areas, albedo, geometry):
    smem = pl.BlockSpec(memory_space=pltpu.SMEM)
    vmem = pl.BlockSpec(memory_space=pltpu.VMEM)
    values = pltpu.VMEM((TASKS, BANDS, BLK), jnp.bfloat16)
    tile = pltpu.VMEM((TASKS, BLK, BLK), jnp.bfloat16)
    return pl.pallas_call(
        fused_kernel,
        in_specs=[smem] * 6 + [vmem] * 4,
        out_specs=vmem,
        out_shape=jax.ShapeDtypeStruct(emission.shape, jnp.float32),
        scratch_shapes=[
            pltpu.VMEM((BLOCKS, BANDS, BLK), jnp.bfloat16),
            pltpu.VMEM((BLOCKS, BANDS, BLK), jnp.float32),
            pltpu.VMEM((TASKS, BANDS, BLK), jnp.float32),
            pltpu.VMEM((DEVICES * SLOTS, BANDS, BLK), jnp.bfloat16),
            pltpu.VMEM((DEVICES, SLOTS * 6, BLK), jnp.float32),
            pltpu.VMEM((DEVICES, SLOTS * 6, BLK), jnp.float32),
        ]
        + [tile] * CHUNKS
        + [values] * (SWEEPS * CHUNKS)
        + [
            pltpu.SemaphoreType.DMA((PEERS,)),
            pltpu.SemaphoreType.DMA((PEERS,)),
            pltpu.SemaphoreType.DMA((SWEEPS * PEERS,)),
            pltpu.SemaphoreType.DMA((SWEEPS * PEERS,)),
        ],
        compiler_params=pltpu.CompilerParams(
            collective_id=0, has_side_effects=True, vmem_limit_bytes=62 << 20
        ),
        name="fused",
    )(send_index, mine_index, order_index, keep, end_index, has, emission, areas, albedo, geometry)


def on_device(
    emission, positions, normals, areas, material, reflect, pair_local, pair_device, pair_block
):
    grp, dev = lax.axis_index("grp"), lax.axis_index("dev")
    me = grp * 16 + dev
    pairs = pair_local.shape[0]

    target = pair_device[:, 0]
    pair_order = jnp.arange(pairs, dtype=jnp.int32)
    earlier = (target[:, None] == target[None, :]) & (pair_order[None, :] < pair_order[:, None])
    slot = target * 2 + jnp.sum(earlier.astype(jnp.int32), 1)
    code = pair_block * BLOCKS + pair_local
    own = jnp.max(
        jnp.where(
            slot[:, None] == jnp.arange(2 * DEVICES, dtype=jnp.int32)[None, :], code[:, None], -1
        ),
        0,
    )
    everyone = lax.all_gather(own, AXES, axis=0, tiled=False).reshape(DEVICES, DEVICES, 2)
    asked = lax.dynamic_index_in_dim(everyone, me, 1, keepdims=False)
    own = own.reshape(DEVICES, 2)

    steps = np.array(ORDER + [(0, 0, 0, 0)], np.int32).T
    there = peer(grp, dev, steps)
    here = peer(grp, dev, (-steps) % np.array([[4], [2], [4], [4]], np.int32))
    there = there[0] * 16 + there[1]
    here = here[0] * 16 + here[1]
    own_there, asked_there = own[there], asked[there]
    own_here, asked_here = own[here], asked[here]
    send_index = jnp.concatenate([own_there % BLOCKS, asked_there // BLOCKS], 1)
    send_index = jnp.where(jnp.concatenate([own_there, asked_there], 1) >= 0, send_index, 0)
    mine = jnp.concatenate([asked_here // BLOCKS, own_here % BLOCKS], 1)
    mine = jnp.where(jnp.concatenate([asked_here, own_here], 1) >= 0, mine, BLOCKS)
    mine = mine.reshape(CHUNKS, TASKS)

    task = jnp.arange(TASKS, dtype=jnp.int32)
    block = jnp.arange(BLOCKS, dtype=jnp.int32)
    key = mine * TASKS + task
    rank = jnp.sum((key[:, None, :] < key[:, :, None]).astype(jnp.int32), 2)
    at_rank = rank[:, None, :] == task[None, :, None]
    order_index = jnp.sum(jnp.where(at_rank, task[None, None, :], 0), 2)
    sorted_mine = jnp.sum(jnp.where(at_rank, mine[:, None, :], 0), 2)
    keep = jnp.concatenate(
        [jnp.zeros((CHUNKS, 1), bool), sorted_mine[:, 1:] == sorted_mine[:, :-1]], 1
    ).astype(jnp.float32)
    upto = jnp.sum((mine[:, None, :] <= block[None, :, None]).astype(jnp.int32), 2)
    has = jnp.any(mine[:, None, :] == block[None, :, None], 2).astype(jnp.float32)

    class_hot = (
        jnp.arange(reflect.shape[1], dtype=jnp.int32)[:, None] == material[None, :]
    ).astype(jnp.float32)
    albedo = jnp.dot(reflect, class_hot, precision=lax.Precision.HIGHEST)
    geometry = jnp.concatenate([positions, normals, jnp.zeros((2, positions.shape[1]))], 0)
    geometry = geometry.astype(jnp.float32).reshape(8, BLOCKS, BLK).transpose(1, 0, 2)

    return fused(
        send_index.reshape(-1),
        jnp.minimum(mine, BLOCKS - 1).reshape(-1),
        order_index.reshape(-1),
        keep.reshape(-1),
        jnp.maximum(upto - 1, 0).reshape(-1),
        has.reshape(-1),
        emission,
        areas[None, :],
        albedo,
        geometry,
    )


def solution(mesh):
    return jax.shard_map(
        on_device,
        mesh=mesh,
        in_specs=(
            P(None, AXES),
            P(None, AXES),
            P(None, AXES),
            P(AXES),
            P(AXES),
            P(),
            P(AXES),
            P(AXES, None),
            P(AXES),
        ),
        out_specs=P(None, AXES),
        check_vma=False,
    )
```

profile of v0, /device:TPU:5, one launch (start us, length us, event | category | flops | bytes accessed | tf_op | source)
XLA Modules:
  0.0 342.3 jit_solution(17203497630783496292)
XLA Ops:
  0.1 0.6 copy-done.7
  0.8 0.6 copy-done.11
  1.5 0.6 copy-done.13
  2.1 0.2 convert_reduce_fusion.2
  2.5 0.1 reshape.95
  2.7 0.6 gather_fusion.3
  3.3 0.6 gather_fusion
  4.3 0.7 copy-done.2
  5.1 0.7 maximum_bitcast_fusion.geometry
  5.8 50.9 %all-gather.1 = s32[128,1,256]{2,1,0:T(1,128)S(1)} all-gather(s32[1,1,256]{2,1,0:T(1,128)S(1)} %bitcast.25), channel_id=2, replica_groups=mesh['grp'=8,'dev'=16] {'grp','dev'}, dimensions={0}, use_global_device_ids=true | all-gather | bytes 132096 | tf_op jit(solution)/shard_map/all_gather | solution.py:268
  57.0 0.6 gather_fusion.2
  57.6 0.6 gather_fusion.1
  58.8 0.7 min.12.mine_index
  59.6 0.7 select_n.88.send_index
  60.5 0.1 fusion.8
  60.7 0.7 reshape.103.has
  61.3 0.1 convert_reduce_fusion.1
  61.5 0.6 max.9.end_index
  62.1 0.2 convert_reduce_fusion
  62.3 0.8 select_reduce_fusion
  63.2 0.7 convert_bitcast_fusion.keep
  63.9 1.6 convolution_bitcast_fusion.albedo
  65.5 274.5 %fused.1 = f32[64,4096]{1,0:T(8,128)} custom-call(s32[512]{0:T(512)} %select_n.88.send_index, s32[512]{0:T(512)} %min.12.mine_index, s32[512]{0:T(512)} %bitcast.26, f32[512]{0:T(512)} %convert_bitcast_fusion.keep, s32[128]{0:T(128)} %max.9.end_index, f32[128]{0:T(128)} %reshape.103.has, f32[64,4096]{1,0:T(8,128)} %emission.1, f32[1,4096]{1,0:T(1,128)} %bitcast.24, ...), custom_call_target="tpu_custom_call" | custom-call | tf_op jit(solution)/shard_map/fused/pallas_call | solution.py:222
  340.0 2.3 copy.48
  (56 shorter events, 1.9 us)
Async XLA Ops:
  0.0 63.9 %copy-start = (f32[64,16]{0,1:T(8,128)S(1)}, f32[64,16]{0,1:T(8,128)}, u32[]{:S(2)}) copy-start(f32[64,16]{0,1:T(8,128)} %param.22) | copy-start | bytes 12292
  0.0 0.7 copy-start.7
  0.0 0.7 copy-start.8
  0.0 0.7 copy-start.9
  0.0 0.7 copy-start.10
  0.0 0.7 copy-start.4
  0.1 0.7 copy-start.5
  0.1 0.7 copy-start.6
  0.8 0.7 copy-start.11
  0.8 0.7 copy-start.12
  1.5 0.7 copy-start.13
  4.2 0.9 copy-start.2
  4.3 0.8 copy-start.1
  61.5 2.4 copy-start.3
where the time goes:
time: 343 us; the launch traced here: 342 us
  Pallas kernels  275 us (80%)
  blocking collectives  50.9 us (15%)
  local copies, waits for them, and re-layouts  11.7 us (3%)
    pallas_call x1, Pallas kernels, fused(): pl.pallas_call(fused_kernel, in_specs=[smem] * 6 + [vmem] * 4, out_specs=...  275 us
    all_gather x1, blocking collectives, on_device(): lax.all_gather(own, AXES, axis=0, tiled=False).reshape(DEVICES, DEVICES, 2)  50.9 us

commit v1 on v0

v1 whole, which is shorter than its diff:
```python
import math

import jax
import jax.numpy as jnp
import numpy as np
from jax import lax
from jax.experimental import pallas as pl
from jax.experimental.pallas import tpu as pltpu
from jax.sharding import PartitionSpec as P

BLK = 128
SWEEPS = 2
AXES = ("grp", "dev")
DEVICES = 128
BLOCKS = 32
BANDS = 64
SLOTS = 4
CHUNKS = 4
PLACES = DEVICES // CHUNKS
TASKS = PLACES * SLOTS
MESH = pl.DeviceIdType.MESH
softening = 0.5


def torus_order():
    seen = set()
    groups = []
    for dx in range(4):
        for dy in range(4):
            for dz in range(4):
                for core in range(2):
                    group = []
                    for x, y, z in ((dx, dy, dz), (dy, dz, dx), (dz, dx, dy)):
                        for step in ((x, core, y, z), (-x % 4, core, -y % 4, -z % 4)):
                            if step not in seen and any(step):
                                seen.add(step)
                                group.append(step)
                    if group:
                        groups.append(group)
    groups.sort(key=lambda group: sum(min(v, 4 - v) for v in group[0][:1] + group[0][2:]))
    return [step for group in groups for step in group]


ORDER = torus_order()
PEERS = len(ORDER)


def peer(grp, dev, step):
    x, core, y, z = step
    return (
        lax.rem(grp // 2 + x, 4) * 2 + lax.rem(lax.rem(grp, 2) + core, 2),
        lax.rem(dev // 4 + y, 4) * 4 + lax.rem(lax.rem(dev, 4) + z, 4),
    )


def opposite(step):
    x, core, y, z = step
    return (-x % 4, core, -y % 4, -z % 4)


BACK = [ORDER.index(opposite(step)) for step in ORDER] + [PEERS]


def turned(step):
    x, core, y, z = step
    return (y, core, z, x)


TURNS = [list(range(PEERS)), [ORDER.index(turned(step)) for step in ORDER]]


def route(asked, owned, out):
    row = lax.broadcasted_iota(jnp.int32, (BLK, BLK), 0)
    lane = lax.broadcasted_iota(jnp.int32, (BLK, BLK), 1)
    lane_row = lane[:1]
    asked0, asked1, owned0, owned1 = asked[0:1], asked[1:2], owned[0:1], owned[1:2]
    mine_rows = [
        jnp.where(asked0 >= 0, asked0 >> 5, BLOCKS),
        jnp.where(asked1 >= 0, asked1 >> 5, BLOCKS),
        jnp.where(owned0 >= 0, owned0 & (BLOCKS - 1), BLOCKS),
        jnp.where(owned1 >= 0, owned1 & (BLOCKS - 1), BLOCKS),
    ]
    place_row = lane_row // PLACES
    for chunk in range(CHUNKS):
        mine = jnp.zeros((1, BLK), jnp.int32)
        for slot in range(SLOTS):
            whole = jnp.broadcast_to(mine_rows[slot], (8, BLK))
            shifted = pltpu.roll(whole, (slot - chunk) * PLACES % BLK, 1)[:1]
            mine = jnp.where(place_row == slot, shifted, mine)
        key = (mine * BLK + lane_row).astype(jnp.float32)
        key_lane = jnp.broadcast_to(key, (BLK, BLK))
        rank = jnp.sum(jnp.where(key_lane.T < key_lane, 1.0, 0.0), 0, keepdims=True)
        at_rank = jnp.broadcast_to(rank, (BLK, BLK)).T == lane.astype(jnp.float32)
        place = ((row % PLACES) * SLOTS + row // PLACES).astype(jnp.float32)
        order = jnp.sum(jnp.where(at_rank, place, 0.0), 0, keepdims=True)
        mine_down = jnp.broadcast_to(mine.astype(jnp.float32), (BLK, BLK)).T
        sorted_mine = jnp.sum(jnp.where(at_rank, mine_down, 0.0), 0, keepdims=True)
        before = pltpu.roll(jnp.broadcast_to(sorted_mine, (8, BLK)), 1, 1)[:1]
        keep = jnp.where((sorted_mine == before) & (lane_row > 0), 1.0, 0.0)
        block = lane.astype(jnp.float32)
        upto = jnp.sum(jnp.where(mine_down <= block, 1.0, 0.0), 0, keepdims=True)
        has = jnp.sum(jnp.where(mine_down == block, 1.0, 0.0), 0, keepdims=True)
        rows = [
            order,
            keep,
            jnp.maximum(upto - 1.0, 0.0),
            jnp.minimum(has, 1.0),
            jnp.minimum(mine, BLOCKS - 1).astype(jnp.float32),
            jnp.zeros((3, BLK), jnp.float32),
        ]
        out[chunk * 8 : chunk * 8 + 8] = jnp.concatenate(rows, 0).astype(jnp.int32)
    asked = jnp.concatenate(
        [jnp.where(asked0 >= 0, asked0 >> 5, 0), jnp.where(asked1 >= 0, asked1 >> 5, 0)]
        + [jnp.zeros((6, BLK), jnp.int32)],
        0,
    )
    out[CHUNKS * 8 : CHUNKS * 8 + 8] = asked


def fused_kernel(
    near_index,
    near_code,
    owned,
    emission,
    areas,
    albedo,
    geometry,
    out,
    scaled,
    total,
    running,
    send,
    near_send,
    near_recv,
    far_send,
    far_recv,
    asked_rows,
    table_rows,
    table,
    tiles0,
    tiles1,
    tiles2,
    tiles3,
    recv00,
    recv01,
    recv02,
    recv03,
    recv10,
    recv11,
    recv12,
    recv13,
    send_sem,
    recv_sem,
    table_sem,
):
    tiles = (tiles0, tiles1, tiles2, tiles3)
    recv = ((recv00, recv01, recv02, recv03), (recv10, recv11, recv12, recv13))
    grp, dev = lax.axis_index("grp"), lax.axis_index("dev")
    core = lax.rem(grp, 2)
    peers = [peer(grp, dev, step) for step in ORDER]
    barrier = pltpu.get_barrier_semaphore()
    for other in peers:
        pl.semaphore_signal(barrier, inc=1, device_id=other, device_id_type=MESH)

    def exchange(kind, source, target):
        copies = [
            pltpu.make_async_remote_copy(
                src_ref=source(place),
                dst_ref=target(place),
                send_sem=send_sem.at[kind * PEERS + place],
                recv_sem=recv_sem.at[kind * PEERS + place],
                device_id=other,
                device_id_type=MESH,
            )
            for place, other in enumerate(peers)
        ]
        for turn in range(2):

            @pl.when(core == turn)
            def _():
                for place in TURNS[turn]:
                    copies[place].start()

        return copies

    def values(sweep, first, count):
        def source(place):
            return send.at[pl.ds(place * SLOTS + first, count)]

        def target(place):
            chunk = recv[sweep][place // PLACES]
            return chunk.at[pl.ds(place % PLACES * SLOTS + first, count)]

        return source, target

    lane = lax.broadcasted_iota(jnp.int32, (4, BLK), 1)

    def pack_near(place, _):
        codes = jnp.where(
            lane == 0,
            near_code[place * 2],
            jnp.where(lane == 1, near_code[place * 2 + 1], 0.0),
        )
        rows = [geometry[near_index[place * 2 + slot]][:6] for slot in range(2)]
        near_send[place] = jnp.concatenate(rows + [codes], 0)
        return 0

    lax.fori_loop(0, DEVICES, pack_near, 0)
    near_recv[PEERS] = near_send[PEERS]
    for block in range(BLOCKS):
        lanes = pl.ds(block * BLK, BLK)
        scaled[block] = (emission[:, lanes] * areas[:, lanes]).astype(jnp.bfloat16)

    def pack_near_values(place, _):
        for slot in range(2):
            send[place * SLOTS + slot] = scaled[near_index[place * 2 + slot]]
        return 0

    lax.fori_loop(0, DEVICES, pack_near_values, 0)
    pl.semaphore_wait(barrier, PEERS)
    near_copies = exchange(0, lambda place: near_send.at[place], lambda place: near_recv.at[place])
    value_copies = exchange(2, *values(0, 0, 2))

    for copy in near_copies:
        copy.wait_recv()

    def collect(place, _):
        asked_rows[pl.ds(place, 1)] = near_recv[place, 12:13]
        return 0

    lax.fori_loop(0, DEVICES, collect, 0)
    route(asked_rows[...].T[:8].astype(jnp.int32), owned[...], table_rows)
    to_table = pltpu.make_async_copy(table_rows, table, table_sem)
    to_table.start()
    to_table.wait()

    def far_index(place, slot):
        return table[CHUNKS * 8 + slot, BACK[place]] & (BLOCKS - 1)

    def pack_far_values():
        for place in range(DEVICES):
            for slot in range(2):
                send[place * SLOTS + 2 + slot] = scaled[far_index(place, slot)]

    for place in range(DEVICES):
        rows = [geometry[far_index(place, slot)][:6] for slot in range(2)]
        far_send[place] = jnp.concatenate(rows + [jnp.zeros((4, BLK), jnp.float32)], 0)
    far_recv[PEERS] = far_send[PEERS]
    far_copies = exchange(1, lambda place: far_send.at[place], lambda place: far_recv.at[place])
    pack_far_values()
    for slot in range(SLOTS):
        recv[0][CHUNKS - 1][TASKS - SLOTS + slot] = send[PEERS * SLOTS + slot]
    far_value_copies = exchange(3, *values(0, 2, 2))

    def build_tiles(chunk, source, first):
        def build(place, _):
            far_all = source[chunk * PLACES + place].T
            for slot in range(2):
                near = geometry[table[chunk * 8 + 4, (first + slot) * PLACES + place] & (BLOCKS - 1)]
                distance_sq = softening
                facing_near = 0.0
                facing_far = 0.0
                for axis in range(3):
                    column = slot * 6 + axis
                    offset = far_all[:, column : column + 1] - near[axis : axis + 1]
                    distance_sq = distance_sq + offset * offset
                    facing_near = facing_near + near[3 + axis : 4 + axis] * offset
                    facing_far = facing_far - far_all[:, column + 3 : column + 4] * offset
                tiles[chunk][place * SLOTS + first + slot] = (
                    jnp.maximum(facing_near, 0.0)
                    * jnp.maximum(facing_far, 0.0)
                    / (math.pi * distance_sq * distance_sq)
                ).astype(jnp.bfloat16)
            return 0

        lax.fori_loop(0, PLACES, build, 0)

    for chunk in range(CHUNKS):
        build_tiles(chunk, near_recv, 0)
    for chunk in range(CHUNKS):
        for copy in far_copies[chunk * PLACES : (chunk + 1) * PLACES]:
            copy.wait_recv()
        build_tiles(chunk, far_recv, 2)

    for sweep in range(SWEEPS):
        if sweep == 0:
            rounds = [value_copies, far_value_copies]
        else:
            for copy in value_copies + far_value_copies:
                copy.wait_send()

            def pack_all_near(place, _):
                for slot in range(2):
                    send[place * SLOTS + slot] = scaled[near_index[place * 2 + slot]]
                return 0

            lax.fori_loop(0, DEVICES, pack_all_near, 0)
            pack_far_values()
            for slot in range(SLOTS):
                recv[1][CHUNKS - 1][TASKS - SLOTS + slot] = send[PEERS * SLOTS + slot]
            rounds = [exchange(4, *values(1, 0, SLOTS))]

        for chunk in range(CHUNKS):
            for copies in rounds:
                for copy in copies[chunk * PLACES : (chunk + 1) * PLACES]:
                    copy.wait_recv()

            def add(group, run):
                for inner in range(8):
                    task = group * 8 + inner
                    index = table[chunk * 8, task] & (TASKS - 1)
                    run = run * table[chunk * 8 + 1, task].astype(jnp.float32) + jnp.dot(
                        recv[sweep][chunk][index],
                        tiles[chunk][index],
                        preferred_element_type=jnp.float32,
                    )
                    running[task] = run
                return run

            lax.fori_loop(0, TASKS // 8, add, jnp.zeros((BANDS, BLK), jnp.float32))

            def fold(block, _):
                part = running[table[chunk * 8 + 2, block] & (TASKS - 1)]
                part = part * table[chunk * 8 + 3, block].astype(jnp.float32)
                total[block] = part if chunk == 0 else total[block] + part
                return 0

            lax.fori_loop(0, BLOCKS, fold, 0)

        for block in range(BLOCKS):
            lanes = pl.ds(block * BLK, BLK)
            current = emission[:, lanes] + albedo[:, lanes] * total[block]
            if sweep + 1 < SWEEPS:
                scaled[block] = (current * areas[:, lanes]).astype(jnp.bfloat16)
            else:
                out[:, lanes] = current
    for copy in near_copies + far_copies + rounds[0]:
        copy.wait_send()


def fused(near_index, near_code, owned, emission, areas, albedo, geometry):
    smem = pl.BlockSpec(memory_space=pltpu.SMEM)
    vmem = pl.BlockSpec(memory_space=pltpu.VMEM)
    values = pltpu.VMEM((TASKS, BANDS, BLK), jnp.bfloat16)
    tile = pltpu.VMEM((TASKS, BLK, BLK), jnp.bfloat16)
    message = pltpu.VMEM((DEVICES, 16, BLK), jnp.float32)
    return pl.pallas_call(
        fused_kernel,
        in_specs=[smem] * 2 + [vmem] * 5,
        out_specs=vmem,
        out_shape=jax.ShapeDtypeStruct(emission.shape, jnp.float32),
        scratch_shapes=[
            pltpu.VMEM((BLOCKS, BANDS, BLK), jnp.bfloat16),
            pltpu.VMEM((BLOCKS, BANDS, BLK), jnp.float32),
            pltpu.VMEM((TASKS, BANDS, BLK), jnp.float32),
            pltpu.VMEM((DEVICES * SLOTS, BANDS, BLK), jnp.bfloat16),
            message,
            message,
            message,
            message,
            pltpu.VMEM((DEVICES, BLK), jnp.float32),
            pltpu.VMEM((CHUNKS * 8 + 8, BLK), jnp.int32),
            pltpu.SMEM((CHUNKS * 8 + 8, BLK), jnp.int32),
        ]
        + [tile] * CHUNKS
        + [values] * (SWEEPS * CHUNKS)
        + [
            pltpu.SemaphoreType.DMA((5 * PEERS,)),
            pltpu.SemaphoreType.DMA((5 * PEERS,)),
            pltpu.SemaphoreType.DMA,
        ],
        compiler_params=pltpu.CompilerParams(
            collective_id=0, has_side_effects=True, vmem_limit_bytes=62 << 20
        ),
        name="fused",
    )(near_index, near_code, owned, emission, areas, albedo, geometry)


def on_device(
    emission, positions, normals, areas, material, reflect, pair_local, pair_device, pair_block
):
    grp, dev = lax.axis_index("grp"), lax.axis_index("dev")
    pairs = pair_local.shape[0]

    target = pair_device[:, 0]
    pair_order = jnp.arange(pairs, dtype=jnp.int32)
    earlier = (target[:, None] == target[None, :]) & (pair_order[None, :] < pair_order[:, None])
    slot = target * 2 + jnp.sum(earlier.astype(jnp.int32), 1)
    code = pair_block * BLOCKS + pair_local
    own = jnp.max(
        jnp.where(
            slot[:, None] == jnp.arange(2 * DEVICES, dtype=jnp.int32)[None, :], code[:, None], -1
        ),
        0,
    )
    own = own.reshape(DEVICES, 2)

    steps = np.array(ORDER + [(0, 0, 0, 0)], np.int32).T
    there = peer(grp, dev, steps)
    here = peer(grp, dev, (-steps) % np.array([[4], [2], [4], [4]], np.int32))
    own_there = own[there[0] * 16 + there[1]]
    own_here = own[here[0] * 16 + here[1]]
    near_index = jnp.where(own_there >= 0, own_there % BLOCKS, 0)
    owned = jnp.concatenate([own_here.T, jnp.zeros((6, DEVICES), jnp.int32)], 0)

    class_hot = (
        jnp.arange(reflect.shape[1], dtype=jnp.int32)[:, None] == material[None, :]
    ).astype(jnp.float32)
    albedo = jnp.dot(reflect, class_hot, precision=lax.Precision.HIGHEST)
    geometry = jnp.concatenate([positions, normals, jnp.zeros((2, positions.shape[1]))], 0)
    geometry = geometry.astype(jnp.float32).reshape(8, BLOCKS, BLK).transpose(1, 0, 2)

    return fused(
        near_index.reshape(-1),
        own_there.astype(jnp.float32).reshape(-1),
        owned,
        emission,
        areas[None, :],
        albedo,
        geometry,
    )


def solution(mesh):
    return jax.shard_map(
        on_device,
        mesh=mesh,
        in_specs=(
            P(None, AXES),
            P(None, AXES),
            P(None, AXES),
            P(AXES),
            P(AXES),
            P(),
            P(AXES),
            P(AXES, None),
            P(AXES),
        ),
        out_specs=P(None, AXES),
        check_vma=False,
    )
```

time: 343 us -> 285 us (0.83)
  the two profiles are of different devices: /device:TPU:5 before, /device:TPU:1 now
where the time goes in v1:
time: 285 us
  Pallas kernels  275 us (96%)
  local copies, waits for them, and re-layouts  6.61 us (2%)
    pallas_call x1, Pallas kernels, fused(): pl.pallas_call(fused_kernel, in_specs=[smem] * 2 + [vmem] * 5, out_specs=...  275 us

profile of v1, /device:TPU:1, one launch (start us, length us, event | category | flops | bytes accessed | tf_op | source)
XLA Modules:
  0.0 284.8 jit_solution(2774498568805938839)
XLA Ops:
  0.1 0.6 copy-done.7
  0.7 0.0 copy-done.8
  0.7 0.0 copy-done.9
  0.7 0.0 copy-done.10
  0.7 0.0 copy-done.4
  0.7 0.0 copy-done.5
  0.8 0.0 copy-done.6
  0.8 0.6 copy-done.11
  1.4 0.0 copy-done.12
  1.5 0.6 copy-done.13
  2.1 0.2 convert_reduce_fusion
  2.3 0.1 select_reduce_fusion
  2.4 0.1 pad.3.clone
  2.5 0.1 reshape.14
  2.7 0.6 gather_fusion.1
  3.3 0.1 copy.20
  3.4 0.7 gather_fusion
  4.0 0.1 gather.9
  4.2 0.6 fusion.23
  4.8 0.6 concatenate.6.owned
  5.4 0.7 maximum_bitcast_fusion.geometry
  6.1 1.6 convolution_bitcast_fusion.albedo
  7.7 274.8 %fused.1 = f32[64,4096]{1,0:T(8,128)} custom-call(s32[256]{0:T(256)} %get-tuple-element.6.near_index, f32[256]{0:T(256)} %get-tuple-element.5.near_code, s32[8,128]{1,0:T(8,128)} %concatenate.6.owned, f32[64,4096]{1,0:T(8,128)} %emission.1, f32[1,4096]{1,0:T(1,128)} %bitcast.16, f32[64,4096]{1,0:T(8,128)} %convolution_bitcast_fusion.albedo, ...), custom_call_target="tpu_custom_call" | custom-call | tf_op jit(solution)/shard_map/fused/pallas_call | solution.py:347
  282.5 2.3 copy.22
  (23 shorter events, 0.1 us)
Async XLA Ops:
  0.0 6.1 %copy-start = (f32[64,16]{0,1:T(8,128)S(1)}, f32[64,16]{0,1:T(8,128)}, u32[]{:S(2)}) copy-start(f32[64,16]{0,1:T(8,128)} %param.22) | copy-start | bytes 12292
  0.0 0.7 copy-start.7
  0.0 0.7 copy-start.8
  0.0 0.7 copy-start.9
  0.0 0.7 copy-start.10
  0.0 0.7 copy-start.4
  0.1 0.7 copy-start.5
  0.1 0.7 copy-start.6
  0.8 0.7 copy-start.11
  0.8 0.7 copy-start.12
  1.5 0.7 copy-start.13
  3.4 2.0 copy-start.2
  4.0 1.3 copy-start.1
  5.4 0.7 copy-start.3
